TPU v7x, 32 devices: a whole 2x2x4 slice. The times are simulated.
32 devices in a mesh: seq: 8 (over z, y), mp: 4 (over x, core).
Axes of the slice: x: 2, y: 2, z: 4, core: 2. Of those that a mesh axis runs over, the one named last changes fastest.
Arguments:
- queries: bfloat16 [3072, 2048], P('seq', 'mp'), may hold values from -110 to 110
- self_keys: bfloat16 [3072, 2048], P('seq', 'mp'), may hold values from -6 to 6
- self_values: bfloat16 [3072, 2048], P('seq', 'mp'), may hold values from -6 to 6
- cross_query: bfloat16 [3072, 2048], P('seq', 'mp'), may hold values from -110 to 110
- memory_keys: bfloat16 [64, 128, 2048], P('seq', None, 'mp'), may hold values from -6 to 6
- memory_values: bfloat16 [64, 128, 2048], P('seq', None, 'mp'), may hold values from -6 to 6
- neighbour_owner: int32 [48, 2], P('seq'), may hold values from 0 to 7, all different within a row; in each aligned block of 6 rows (0 to 5, 6 to 11, ...) at most 2 rows name the same one
- neighbour_slot: int32 [48, 2], P('seq'), may hold values from 0 to 7
- out_weight: bfloat16 [2048, 4096], P('mp'), may hold values from -0.125 to 0.125
- cross_weight: bfloat16 [2048, 4096], P('mp'), may hold values from -0.125 to 0.125
Outputs:
- block_out: bfloat16 [3072, 4096], P('seq', 'mp')
Inputs may be any that keep to these rules, and one draw needn't show every extreme that they name: `neighbour_owner`: the 2 neighbours of a span have different owners; among the spans of one index of seq, at most 2 neighbours have one owner.
All inputs are finite; a program needn't handle non-finite values.
Results may differ from a plain program's by a relative error of at most 0.025.
Values may be sent and summed in bfloat16 or wider, within the bound.
A program may use at most 128 MiB of HBM per device.

v0:
```python
import jax
import jax.numpy as jnp
from jax import lax
from jax.sharding import PartitionSpec as P

HEAD = 128
SPAN = 64
NEG_FILL = -1e30


def from_behind(value, axis, steps):
    count = lax.axis_size(axis)
    leading, last = (max(0, -steps), min(count, count - steps))
    return lax.ppermute(value, axis, [(source, source + steps) for source in range(leading, last)])


def split_heads(matrix_block, head_width):
    return matrix_block.reshape(
        matrix_block.shape[:-1] + (matrix_block.shape[-1] // head_width, head_width)
    )


def attend_block(carried, queries, key_value, causal):
    running, totals, numerator = carried
    query_heads = split_heads(queries, HEAD)
    key_heads = split_heads(key_value[0], HEAD)
    value_heads = split_heads(key_value[1], HEAD)
    scores = jnp.einsum(
        "tha,uha->htu", query_heads, key_heads, preferred_element_type=jnp.float32
    ) * HEAD ** (-0.5)
    row_count = queries.shape[0]
    causal_ok = lax.broadcasted_iota(jnp.int32, (row_count, row_count), 0) >= lax.broadcasted_iota(
        jnp.int32, (row_count, row_count), 1
    )
    allowed = jnp.logical_or(causal_ok, jnp.logical_not(causal))
    masked = jnp.where(allowed[None], scores, NEG_FILL)
    newest = jnp.maximum(running, jnp.max(masked, axis=2))
    weights = jnp.exp(masked - newest[..., None])
    factor = jnp.exp(running - newest)
    totals = totals * factor + jnp.sum(weights, axis=2)
    numerator = numerator * factor[..., None] + jnp.einsum(
        "htu,uha->hta",
        weights.astype(jnp.bfloat16),
        value_heads,
        preferred_element_type=jnp.float32,
    )
    return (newest, totals, numerator)


def visit(carried, queries, key_value, source, own_index):
    return lax.cond(
        source < own_index,
        lambda status: attend_block(status, queries, key_value, False),
        lambda status: status,
        carried,
    )


def pass_lower(key_value):
    return from_behind(key_value, "seq", 1)


def self_attention(queries, self_keys, self_values):
    devices = lax.axis_size("seq")
    own_index = lax.axis_index("seq")
    row_count = queries.shape[0]
    heads_here = queries.shape[1] // HEAD
    key_value = jnp.stack([self_keys, self_values])
    initial = (
        jnp.full((heads_here, row_count), NEG_FILL, jnp.float32),
        jnp.zeros((heads_here, row_count), jnp.float32),
        jnp.zeros((heads_here, row_count, HEAD), jnp.float32),
    )
    carried = attend_block(initial, queries, key_value, True)

    def one_way(turn_index, status):
        travel, inner_state = status
        travel = pass_lower(travel)
        return (
            travel,
            visit(inner_state, queries, travel, (own_index - turn_index) % devices, own_index),
        )

    travel, carried = lax.fori_loop(1, devices, one_way, (key_value, carried))
    running, totals, numerator = carried
    blended = numerator / totals[..., None]
    return (
        jnp.transpose(blended, (1, 0, 2)).reshape(row_count, heads_here * HEAD).astype(jnp.bfloat16)
    )


def cross_attention(cross_query, memory_keys, memory_values, neighbour_owner, neighbour_slot):
    devices = lax.axis_size("seq")
    span_count = neighbour_owner.shape[0]
    pick_count = neighbour_owner.shape[1]
    request_count = span_count * pick_count
    capacity = max(2, (request_count + devices - 1) // devices)
    slot_total = devices * capacity
    feature_count = cross_query.shape[1]
    heads_here = feature_count // HEAD
    owner_list = neighbour_owner.reshape(request_count)
    slot_list = neighbour_slot.reshape(request_count)
    owner_hits = (owner_list[:, None] == jnp.arange(devices, dtype=jnp.int32)[None, :]).astype(
        jnp.int32
    )
    earlier = jnp.cumsum(owner_hits, axis=0) - owner_hits
    rank_within = jnp.sum(earlier * owner_hits, axis=1)
    target_slot = owner_list * capacity + rank_within
    routing = target_slot[:, None] == jnp.arange(slot_total, dtype=jnp.int32)[None, :]
    span_rows = cross_query.reshape(span_count, SPAN * feature_count)
    request_rows = jnp.repeat(span_rows, pick_count, axis=0)
    outgoing = jnp.dot(
        jnp.transpose(routing).astype(jnp.bfloat16),
        request_rows,
        preferred_element_type=jnp.float32,
    ).astype(jnp.bfloat16)
    outgoing = outgoing.reshape(devices, capacity, SPAN, feature_count)
    asked_slots = jnp.sum(jnp.where(routing, slot_list[:, None], 0), axis=0).reshape(
        devices, capacity
    )
    asked = lax.all_to_all(outgoing, "seq", split_axis=0, concat_axis=0, tiled=True)
    wanted = lax.all_to_all(asked_slots, "seq", split_axis=0, concat_axis=0, tiled=True)
    source_count = wanted.shape[0]
    item_count = wanted.shape[1]
    key_heads = split_heads(memory_keys[wanted], HEAD)
    value_heads = split_heads(memory_values[wanted], HEAD)
    query_heads = split_heads(asked, HEAD)
    scores = jnp.einsum(
        "nicha,nikha->nihck", query_heads, key_heads, preferred_element_type=jnp.float32
    ) * HEAD ** (-0.5)
    highest = jnp.max(scores, axis=4)
    weights = jnp.exp(scores - highest[..., None])
    totals = jnp.sum(weights, axis=4)
    blended = jnp.einsum(
        "nihck,nikha->nicha",
        weights.astype(jnp.bfloat16),
        value_heads,
        preferred_element_type=jnp.float32,
    )
    blended = blended / jnp.transpose(totals, (0, 1, 3, 2))[..., None]
    answer = blended.reshape(source_count, item_count, SPAN, feature_count).astype(jnp.bfloat16)
    log_mass = highest + jnp.log(totals)
    answers = lax.all_to_all(answer, "seq", split_axis=0, concat_axis=0, tiled=True)
    log_masses = lax.all_to_all(
        log_mass.astype(jnp.bfloat16), "seq", split_axis=0, concat_axis=0, tiled=True
    ).astype(log_mass.dtype)
    answer_rows = jnp.dot(
        routing.astype(jnp.bfloat16),
        answers.reshape(slot_total, SPAN * feature_count),
        preferred_element_type=jnp.float32,
    )
    mass_rows = jnp.dot(
        routing.astype(jnp.float32),
        log_masses.reshape(slot_total, heads_here * SPAN),
        precision=lax.Precision.HIGHEST,
    )
    answer_rows = answer_rows.reshape(span_count, pick_count, SPAN, heads_here, HEAD)
    mass_rows = mass_rows.reshape(span_count, pick_count, heads_here, SPAN)
    best_mass = jnp.max(mass_rows, axis=1, keepdims=True)
    shares = jnp.exp(mass_rows - best_mass)
    share_cols = jnp.transpose(shares, (0, 1, 3, 2))[..., None]
    combined = jnp.sum(share_cols * answer_rows, axis=1) / jnp.sum(share_cols, axis=1)
    return combined.reshape(span_count * SPAN, feature_count).astype(jnp.bfloat16)


def per_device(
    queries,
    self_keys,
    self_values,
    cross_query,
    memory_keys,
    memory_values,
    neighbour_owner,
    neighbour_slot,
    out_weight,
    cross_weight,
):
    attended = self_attention(queries, self_keys, self_values)
    retrieved = cross_attention(
        cross_query, memory_keys, memory_values, neighbour_owner, neighbour_slot
    )
    partial_value = jnp.dot(attended, out_weight, preferred_element_type=jnp.float32)
    partial_value = partial_value + jnp.dot(
        retrieved, cross_weight, preferred_element_type=jnp.float32
    )
    return lax.psum_scatter(
        partial_value.astype(jnp.bfloat16), "mp", scatter_dimension=1, tiled=True
    )


def solution(mesh):
    placed = (
        P("seq", "mp"),
        P("seq", "mp"),
        P("seq", "mp"),
        P("seq", "mp"),
        P("seq", None, "mp"),
        P("seq", None, "mp"),
        P("seq", None),
        P("seq", None),
        P("mp", None),
        P("mp", None),
    )
    return jax.shard_map(
        per_device, mesh=mesh, in_specs=placed, out_specs=P("seq", "mp"), check_vma=False
    )
```

profile of v0, /device:TPU:0, one launch (start us, length us, event | category | flops | bytes accessed | tf_op | source)
XLA Modules:
  0.0 320.3 jit_solution(1754445644933671382)
XLA Ops:
  9.3 7.3 %all-to-all-start.1 = ((s32[8,1,2]{2,1,0:T(1,128)}), s32[8,1,2]{2,1,0:T(1,128)S(1)}, u32[]{:S(2)}, u32[]{:S(2)}) async-start(s32[8,1,2]{2,1,0:T(1,128)} %bitcast.9), calls=%async_computation.1 | async-start | bytes 8192 | tf_op jit(solution)/shard_map/all_to_all | solution.py:122
  23.0 4.2 %all-to-all-start = ((bf16[8,2,64,512]{3,2,1,0:T(8,128)(2,1)}), bf16[8,2,64,512]{3,2,1,0:T(8,128)(2,1)}, u32[]{:S(2)}, u32[]{:S(2)}) async-start(bf16[8,2,64,512]{3,2,1,0:T(8,128)(2,1)} %bitcast.39), calls=%async_computation | async-start | bytes 2097152 | tf_op jit(solution)/shard_map/all_to_all | solution.py:121
  40.0 12.4 %all-to-all-done = bf16[8,2,64,512]{3,2,1,0:T(8,128)(2,1)} async-done(((bf16[8,2,64,512]{3,2,1,0:T(8,128)(2,1)}), bf16[8,2,64,512]{3,2,1,0:T(8,128)(2,1)}, u32[]{:S(2)}, u32[]{:S(2)}) %all-to-all-start) | async-done | bytes 1048608 | tf_op jit(solution)/shard_map/all_to_all | solution.py:121
  52.4 3.6 %multiply_reduce_fusion.2 = (f32[8,2,4,64]{3,2,1,0:T(4,128)S(1)}, f32[8,2,4,64,128]{4,3,2,1,0:T(8,128)S(1)}) fusion(bf16[8,2,128,4,128]{4,3,2,1,0:T(4,128)(2,1)} %reshape.152, bf16[8,2,64,512]{3,2,1,0:T(8,128)(2,1)} %all-to-all-done), kind=kOutput, calls=%fused_computation.28 | convolution fusion | flops 135262208 | bytes 5259264 | tf_op jit(solution)/shard_map/nicha,nikha->nihck/dot_general | solution.py:128
  60.0 3.4 %all-to-all-start.2 = ((bf16[8,2,256]{2,1,0:T(2,128)(2,1)}), bf16[8,2,256]{2,1,0:T(2,128)(2,1)S(1)}, u32[]{:S(2)}, u32[]{:S(2)}) async-start(bf16[8,2,256]{2,1,0:T(2,128)(2,1)} %reshape.180), calls=%async_computation.2 | async-start | bytes 16384 | tf_op jit(solution)/shard_map/all_to_all | solution.py:144
  69.8 4.3 %all-to-all-start.3 = ((bf16[8,2,64,512]{3,2,1,0:T(8,128)(2,1)}), bf16[8,2,64,512]{3,2,1,0:T(8,128)(2,1)}, u32[]{:S(2)}, u32[]{:S(2)}) async-start(bf16[8,2,64,512]{3,2,1,0:T(8,128)(2,1)} %bitcast.118), calls=%async_computation.3 | async-start | bytes 2097152 | tf_op jit(solution)/shard_map/all_to_all | solution.py:143
  77.9 163.0 %while.21 = (s32[]{:T(128)}, bf16[2,384,512]{1,2,0:T(8,128)(2,1)}, f32[4,384]{1,0:T(4,128)S(1)}, f32[4,384]{1,0:T(4,128)S(1)}, f32[4,384,128]{2,1,0:T(8,128)S(1)...) while((s32[]{:T(128)}, bf16[2,384,512]{1,2,0:T(8,128)(2,1)}, ...), condition=%wide.region_7.8_spmd, body=%wide.region_2.7_spmd.sunk | while | flops 307104768 | bytes 16220540 | solution.py:84
  77.9 3.6 %collective-permute-start = (bf16[2,384,512]{1,2,0:T(8,128)(2,1)}, bf16[2,384,512]{1,2,0:T(8,128)(2,1)S(1)}, u32[]{:S(2)}, u32[]{:S(2)}) collective-permute-start(bf16[2,384,512]{1,2,0:T(8,128)(2,1)} %get-tuple-element.321), channel_id=1, source_target_pairs={{0,4},{4,8},{8,12},{12,16},{16,20},{20,24},{24,28},{1,5},{5,9},{9,... | collective-permute-start | bytes 2359304 | tf_op jit(solution)/shard_map/while/body/eval_jaxpr/ppermute | solution.py:14
  81.6 19.9 %collective-permute-done = bf16[2,384,512]{1,2,0:T(8,128)(2,1)S(1)} collective-permute-done((bf16[2,384,512]{1,2,0:T(8,128)(2,1)}, bf16[2,384,512]{1,2,0:T(8,128)(2,1)S(1)}, u32[]{:S(2)}, u32[]{:S(2)}) %collective-permute-start) | collective-permute-done | bytes 786464 | tf_op jit(solution)/shard_map/while/body/eval_jaxpr/ppermute | solution.py:14
  102.3 12.8 %collective-permute-start = (bf16[2,384,512]{1,2,0:T(8,128)(2,1)}, bf16[2,384,512]{1,2,0:T(8,128)(2,1)S(1)}, u32[]{:S(2)}, u32[]{:S(2)}) collective-permute-start(bf16[2,384,512]{1,2,0:T(8,128)(2,1)} %get-tuple-element.321), channel_id=1, source_target_pairs={{0,4},{4,8},{8,12},{12,16},{16,20},{20,24},{24,28},{1,5},{5,9},{9,... | collective-permute-start | bytes 2359304 | tf_op jit(solution)/shard_map/while/body/eval_jaxpr/ppermute | solution.py:14
  115.2 14.9 %collective-permute-done = bf16[2,384,512]{1,2,0:T(8,128)(2,1)S(1)} collective-permute-done((bf16[2,384,512]{1,2,0:T(8,128)(2,1)}, bf16[2,384,512]{1,2,0:T(8,128)(2,1)S(1)}, u32[]{:S(2)}, u32[]{:S(2)}) %collective-permute-start) | collective-permute-done | bytes 786464 | tf_op jit(solution)/shard_map/while/body/eval_jaxpr/ppermute | solution.py:14
  131.0 5.2 %collective-permute-start = (bf16[2,384,512]{1,2,0:T(8,128)(2,1)}, bf16[2,384,512]{1,2,0:T(8,128)(2,1)S(1)}, u32[]{:S(2)}, u32[]{:S(2)}) collective-permute-start(bf16[2,384,512]{1,2,0:T(8,128)(2,1)} %get-tuple-element.321), channel_id=1, source_target_pairs={{0,4},{4,8},{8,12},{12,16},{16,20},{20,24},{24,28},{1,5},{5,9},{9,... | collective-permute-start | bytes 2359304 | tf_op jit(solution)/shard_map/while/body/eval_jaxpr/ppermute | solution.py:14
  136.3 14.0 %collective-permute-done = bf16[2,384,512]{1,2,0:T(8,128)(2,1)S(1)} collective-permute-done((bf16[2,384,512]{1,2,0:T(8,128)(2,1)}, bf16[2,384,512]{1,2,0:T(8,128)(2,1)S(1)}, u32[]{:S(2)}, u32[]{:S(2)}) %collective-permute-start) | collective-permute-done | bytes 786464 | tf_op jit(solution)/shard_map/while/body/eval_jaxpr/ppermute | solution.py:14
  151.1 12.3 %collective-permute-start = (bf16[2,384,512]{1,2,0:T(8,128)(2,1)}, bf16[2,384,512]{1,2,0:T(8,128)(2,1)S(1)}, u32[]{:S(2)}, u32[]{:S(2)}) collective-permute-start(bf16[2,384,512]{1,2,0:T(8,128)(2,1)} %get-tuple-element.321), channel_id=1, source_target_pairs={{0,4},{4,8},{8,12},{12,16},{16,20},{20,24},{24,28},{1,5},{5,9},{9,... | collective-permute-start | bytes 2359304 | tf_op jit(solution)/shard_map/while/body/eval_jaxpr/ppermute | solution.py:14
  163.5 15.4 %collective-permute-done = bf16[2,384,512]{1,2,0:T(8,128)(2,1)S(1)} collective-permute-done((bf16[2,384,512]{1,2,0:T(8,128)(2,1)}, bf16[2,384,512]{1,2,0:T(8,128)(2,1)S(1)}, u32[]{:S(2)}, u32[]{:S(2)}) %collective-permute-start) | collective-permute-done | bytes 786464 | tf_op jit(solution)/shard_map/while/body/eval_jaxpr/ppermute | solution.py:14
  179.8 5.2 %collective-permute-start = (bf16[2,384,512]{1,2,0:T(8,128)(2,1)}, bf16[2,384,512]{1,2,0:T(8,128)(2,1)S(1)}, u32[]{:S(2)}, u32[]{:S(2)}) collective-permute-start(bf16[2,384,512]{1,2,0:T(8,128)(2,1)} %get-tuple-element.321), channel_id=1, source_target_pairs={{0,4},{4,8},{8,12},{12,16},{16,20},{20,24},{24,28},{1,5},{5,9},{9,... | collective-permute-start | bytes 2359304 | tf_op jit(solution)/shard_map/while/body/eval_jaxpr/ppermute | solution.py:14
  185.0 14.5 %collective-permute-done = bf16[2,384,512]{1,2,0:T(8,128)(2,1)S(1)} collective-permute-done((bf16[2,384,512]{1,2,0:T(8,128)(2,1)}, bf16[2,384,512]{1,2,0:T(8,128)(2,1)S(1)}, u32[]{:S(2)}, u32[]{:S(2)}) %collective-permute-start) | collective-permute-done | bytes 786464 | tf_op jit(solution)/shard_map/while/body/eval_jaxpr/ppermute | solution.py:14
  200.4 7.2 %collective-permute-start = (bf16[2,384,512]{1,2,0:T(8,128)(2,1)}, bf16[2,384,512]{1,2,0:T(8,128)(2,1)S(1)}, u32[]{:S(2)}, u32[]{:S(2)}) collective-permute-start(bf16[2,384,512]{1,2,0:T(8,128)(2,1)} %get-tuple-element.321), channel_id=1, source_target_pairs={{0,4},{4,8},{8,12},{12,16},{16,20},{20,24},{24,28},{1,5},{5,9},{9,... | collective-permute-start | bytes 2359304 | tf_op jit(solution)/shard_map/while/body/eval_jaxpr/ppermute | solution.py:14
  207.7 13.6 %collective-permute-done = bf16[2,384,512]{1,2,0:T(8,128)(2,1)S(1)} collective-permute-done((bf16[2,384,512]{1,2,0:T(8,128)(2,1)}, bf16[2,384,512]{1,2,0:T(8,128)(2,1)S(1)}, u32[]{:S(2)}, u32[]{:S(2)}) %collective-permute-start) | collective-permute-done | bytes 786464 | tf_op jit(solution)/shard_map/while/body/eval_jaxpr/ppermute | solution.py:14
  222.2 5.2 %collective-permute-start = (bf16[2,384,512]{1,2,0:T(8,128)(2,1)}, bf16[2,384,512]{1,2,0:T(8,128)(2,1)S(1)}, u32[]{:S(2)}, u32[]{:S(2)}) collective-permute-start(bf16[2,384,512]{1,2,0:T(8,128)(2,1)} %get-tuple-element.321), channel_id=1, source_target_pairs={{0,4},{4,8},{8,12},{12,16},{16,20},{20,24},{24,28},{1,5},{5,9},{9,... | collective-permute-start | bytes 2359304 | tf_op jit(solution)/shard_map/while/body/eval_jaxpr/ppermute | solution.py:14
  227.4 12.7 %collective-permute-done = bf16[2,384,512]{1,2,0:T(8,128)(2,1)S(1)} collective-permute-done((bf16[2,384,512]{1,2,0:T(8,128)(2,1)}, bf16[2,384,512]{1,2,0:T(8,128)(2,1)S(1)}, u32[]{:S(2)}, u32[]{:S(2)}) %collective-permute-start) | collective-permute-done | bytes 786464 | tf_op jit(solution)/shard_map/while/body/eval_jaxpr/ppermute | solution.py:14
  241.3 6.7 %fusion.65 = f32[384,4096]{1,0:T(8,128)} fusion(bf16[384,512]{0,1:T(8,128)(2,1)S(1)} %bitcast.128, bf16[512,4096]{1,0:T(8,128)(2,1)} %param.22), kind=kOutput, calls=%fused_computation.89 | convolution fusion | flops 1610612736 | bytes 10878976 | tf_op jit(solution)/shard_map/dot_general | solution.py:182
  258.2 3.6 %add_convert_fusion = bf16[384,4096]{1,0:T(8,128)(2,1)} fusion(f32[384,4096]{1,0:T(8,128)S(1)} %bitcast.122, bf16[512,4096]{1,0:T(8,128)(2,1)S(1)} %copy-done.2, bf16[48,8,4,128]{3,2,1,0:T(4,128)(2,1)S(1)} %bitcast.125), kind=kOutput, calls=%fused_computation.16 | convolution fusion | flops 1613758464 | bytes 14024704 | tf_op jit(solution)/shard_map/dot_general | solution.py:183
  261.8 51.7 %reduce-scatter.2.cloned.1.call-done = bf16[384,1024]{1,0:T(8,128)(2,1)} async-done(((bf16[384,4096]{1,0:T(8,128)(2,1)}), bf16[384,1024]{1,0:T(8,128)(2,1)}) %reduce-scatter.2.cloned.1.call-update) | async-done | bytes 786448 | tf_op jit(solution)/shard_map/reduce_scatter | solution.py:186
  (113 shorter events, 52.6 us)
Async XLA Ops:
  6.5 26.7 %copy-start = (bf16[8,128,512]{2,1,0:T(8,128)(2,1)S(1)}, bf16[8,128,512]{2,1,0:T(8,128)(2,1)}, u32[]{:S(2)}) copy-start(bf16[8,128,512]{2,1,0:T(8,128)(2,1)} %param.19) | copy-start | bytes 3145732
  9.3 13.7 %all-to-all-start.1 = ((s32[8,1,2]{2,1,0:T(1,128)}), s32[8,1,2]{2,1,0:T(1,128)S(1)}, u32[]{:S(2)}, u32[]{:S(2)}) async-start(s32[8,1,2]{2,1,0:T(1,128)} %bitcast.9), calls=%async_computation.1 | async-start | bytes 8192 | tf_op jit(solution)/shard_map/all_to_all | solution.py:122
  19.3 8.6 %copy-start.8 = (bf16[384,512]{1,0:T(8,128)(2,1)S(1)}, bf16[384,512]{1,0:T(8,128)(2,1)}, u32[]{:S(2)}) copy-start(bf16[384,512]{1,0:T(8,128)(2,1)} %param.15) | copy-start | bytes 1179652
  19.4 9.5 %copy-start.9 = (bf16[384,512]{1,0:T(8,128)(2,1)S(1)}, bf16[384,512]{1,0:T(8,128)(2,1)}, u32[]{:S(2)}) copy-start(bf16[384,512]{1,0:T(8,128)(2,1)} %param.16) | copy-start | bytes 1179652
  20.7 9.1 %copy-start.1 = (bf16[384,512]{1,0:T(8,128)(2,1)S(1)}, bf16[384,512]{1,0:T(8,128)(2,1)}, u32[]{:S(2)}) copy-start(bf16[384,512]{1,0:T(8,128)(2,1)} %param.14) | copy-start | bytes 1179652
  23.0 29.4 %all-to-all-start = ((bf16[8,2,64,512]{3,2,1,0:T(8,128)(2,1)}), bf16[8,2,64,512]{3,2,1,0:T(8,128)(2,1)}, u32[]{:S(2)}, u32[]{:S(2)}) async-start(bf16[8,2,64,512]{3,2,1,0:T(8,128)(2,1)} %bitcast.39), calls=%async_computation | async-start | bytes 2097152 | tf_op jit(solution)/shard_map/all_to_all | solution.py:121
  60.0 9.9 %all-to-all-start.2 = ((bf16[8,2,256]{2,1,0:T(2,128)(2,1)}), bf16[8,2,256]{2,1,0:T(2,128)(2,1)S(1)}, u32[]{:S(2)}, u32[]{:S(2)}) async-start(bf16[8,2,256]{2,1,0:T(2,128)(2,1)} %reshape.180), calls=%async_computation.2 | async-start | bytes 16384 | tf_op jit(solution)/shard_map/all_to_all | solution.py:144
  66.0 8.3 %copy-start.4 = (bf16[384,512]{0,1:T(8,128)(2,1)S(1)}, bf16[384,512]{0,1:T(8,128)(2,1)}, u32[]{:S(2)}) copy-start(bf16[384,512]{0,1:T(8,128)(2,1)} %copy.107) | copy-start | bytes 1179652
  66.0 8.3 %copy-start.5 = (bf16[384,512]{0,1:T(8,128)(2,1)S(1)}, bf16[384,512]{0,1:T(8,128)(2,1)}, u32[]{:S(2)}) copy-start(bf16[384,512]{0,1:T(8,128)(2,1)} %copy.108) | copy-start | bytes 1179652
  67.3 8.1 %copy-start.13 = (f32[4,384]{1,0:T(4,128)S(1)}, f32[4,384]{1,0:T(4,128)}, u32[]{:S(2)}) copy-start(f32[4,384]{1,0:T(4,128)} %fusion.16) | copy-start | bytes 18436
  67.3 8.1 %copy-start.15 = (f32[4,384]{1,0:T(4,128)S(1)}, f32[4,384]{1,0:T(4,128)}, u32[]{:S(2)}) copy-start(f32[4,384]{1,0:T(4,128)} %copy-done.14) | copy-start | bytes 18436
  67.3 8.1 %copy-start.7 = (pred[384,384]{0,1:T(8,128)(4,1)S(1)}, pred[384,384]{0,1:T(8,128)(4,1)}, u32[]{:S(2)}) copy-start(pred[384,384]{0,1:T(8,128)(4,1)} %copy-done.6) | copy-start | bytes 442372
  67.3 8.1 %copy-start.10 = (bf16[384,512]{1,0:T(8,128)(2,1)S(1)}, bf16[384,512]{1,0:T(8,128)(2,1)}, u32[]{:S(2)}) copy-start(bf16[384,512]{1,0:T(8,128)(2,1)} %param.16) | copy-start | bytes 1179652
  69.8 179.0 %all-to-all-start.3 = ((bf16[8,2,64,512]{3,2,1,0:T(8,128)(2,1)}), bf16[8,2,64,512]{3,2,1,0:T(8,128)(2,1)}, u32[]{:S(2)}, u32[]{:S(2)}) async-start(bf16[8,2,64,512]{3,2,1,0:T(8,128)(2,1)} %bitcast.118), calls=%async_computation.3 | async-start | bytes 2097152 | tf_op jit(solution)/shard_map/all_to_all | solution.py:143
  74.1 239.4 %reduce-scatter.2.cloned.1.call-start = ((), (), s32[]{:S(2)}) async-start(), calls=%async_computation.5 | async-start | bytes 3932160 | tf_op jit(solution)/shard_map/reduce_scatter | solution.py:186
  77.9 23.5 %collective-permute-start = (bf16[2,384,512]{1,2,0:T(8,128)(2,1)}, bf16[2,384,512]{1,2,0:T(8,128)(2,1)S(1)}, u32[]{:S(2)}, u32[]{:S(2)}) collective-permute-start(bf16[2,384,512]{1,2,0:T(8,128)(2,1)} %get-tuple-element.321), channel_id=1, source_target_pairs={{0,4},{4,8},{8,12},{12,16},{16,20},{20,24},{24,28},{1,5},{5,9},{9,... | collective-permute-start | bytes 2359304 | tf_op jit(solution)/shard_map/while/body/eval_jaxpr/ppermute | solution.py:14
  102.3 27.8 %collective-permute-start = (bf16[2,384,512]{1,2,0:T(8,128)(2,1)}, bf16[2,384,512]{1,2,0:T(8,128)(2,1)S(1)}, u32[]{:S(2)}, u32[]{:S(2)}) collective-permute-start(bf16[2,384,512]{1,2,0:T(8,128)(2,1)} %get-tuple-element.321), channel_id=1, source_target_pairs={{0,4},{4,8},{8,12},{12,16},{16,20},{20,24},{24,28},{1,5},{5,9},{9,... | collective-permute-start | bytes 2359304 | tf_op jit(solution)/shard_map/while/body/eval_jaxpr/ppermute | solution.py:14
  131.0 19.2 %collective-permute-start = (bf16[2,384,512]{1,2,0:T(8,128)(2,1)}, bf16[2,384,512]{1,2,0:T(8,128)(2,1)S(1)}, u32[]{:S(2)}, u32[]{:S(2)}) collective-permute-start(bf16[2,384,512]{1,2,0:T(8,128)(2,1)} %get-tuple-element.321), channel_id=1, source_target_pairs={{0,4},{4,8},{8,12},{12,16},{16,20},{20,24},{24,28},{1,5},{5,9},{9,... | collective-permute-start | bytes 2359304 | tf_op jit(solution)/shard_map/while/body/eval_jaxpr/ppermute | solution.py:14
  151.1 27.8 %collective-permute-start = (bf16[2,384,512]{1,2,0:T(8,128)(2,1)}, bf16[2,384,512]{1,2,0:T(8,128)(2,1)S(1)}, u32[]{:S(2)}, u32[]{:S(2)}) collective-permute-start(bf16[2,384,512]{1,2,0:T(8,128)(2,1)} %get-tuple-element.321), channel_id=1, source_target_pairs={{0,4},{4,8},{8,12},{12,16},{16,20},{20,24},{24,28},{1,5},{5,9},{9,... | collective-permute-start | bytes 2359304 | tf_op jit(solution)/shard_map/while/body/eval_jaxpr/ppermute | solution.py:14
  179.8 19.8 %collective-permute-start = (bf16[2,384,512]{1,2,0:T(8,128)(2,1)}, bf16[2,384,512]{1,2,0:T(8,128)(2,1)S(1)}, u32[]{:S(2)}, u32[]{:S(2)}) collective-permute-start(bf16[2,384,512]{1,2,0:T(8,128)(2,1)} %get-tuple-element.321), channel_id=1, source_target_pairs={{0,4},{4,8},{8,12},{12,16},{16,20},{20,24},{24,28},{1,5},{5,9},{9,... | collective-permute-start | bytes 2359304 | tf_op jit(solution)/shard_map/while/body/eval_jaxpr/ppermute | solution.py:14
  200.4 20.8 %collective-permute-start = (bf16[2,384,512]{1,2,0:T(8,128)(2,1)}, bf16[2,384,512]{1,2,0:T(8,128)(2,1)S(1)}, u32[]{:S(2)}, u32[]{:S(2)}) collective-permute-start(bf16[2,384,512]{1,2,0:T(8,128)(2,1)} %get-tuple-element.321), channel_id=1, source_target_pairs={{0,4},{4,8},{8,12},{12,16},{16,20},{20,24},{24,28},{1,5},{5,9},{9,... | collective-permute-start | bytes 2359304 | tf_op jit(solution)/shard_map/while/body/eval_jaxpr/ppermute | solution.py:14
  222.2 17.9 %collective-permute-start = (bf16[2,384,512]{1,2,0:T(8,128)(2,1)}, bf16[2,384,512]{1,2,0:T(8,128)(2,1)S(1)}, u32[]{:S(2)}, u32[]{:S(2)}) collective-permute-start(bf16[2,384,512]{1,2,0:T(8,128)(2,1)} %get-tuple-element.321), channel_id=1, source_target_pairs={{0,4},{4,8},{8,12},{12,16},{16,20},{20,24},{24,28},{1,5},{5,9},{9,... | collective-permute-start | bytes 2359304 | tf_op jit(solution)/shard_map/while/body/eval_jaxpr/ppermute | solution.py:14
  241.3 7.0 %copy-start.16 = (s32[6,2]{0,1:T(2,128)S(1)}, s32[6,2]{0,1:T(2,128)}, u32[]{:S(2)}) copy-start(s32[6,2]{0,1:T(2,128)} %copy.116) | copy-start | bytes 148
  251.6 5.8 %slice-start = ((s8[6291456]{0:T(1024)(128)(4,1)}), s8[2097152]{0:T(1024)(128)(4,1)S(1)}, s32[]{:S(2)}) async-start(s8[6291456]{0:T(1024)(128)(4,1)} %bitcast.121), calls=%async_computation.6 | async-start | bytes 4194304
  (7 other events, 16.1 us)
Sparse Core Ops, SparseCore 0:
  261.9 51.5 reduce-scatter.1
where the time goes:
time: 321 us; the launch traced here: 320 us
  waiting for transfers between devices  174 us (54%)
  starting transfers between devices  71 us (22%)
  local copies, waits for them, and re-layouts  33.6 us (10%)
  matrix products  22.9 us (7%)
  between operations  13.7 us (4%)
  other arithmetic  4.82 us (2%)
    ppermute x7, waiting for transfers between devices, from_behind(): lax.ppermute(value, axis, [(source, source + steps) for source in range(l...  105 us
    reduce_scatter x1, waiting for transfers between devices, per_device(): lax.psum_scatter(partial_value.astype(jnp.bfloat16), 'mp', scatter_dimens...  51.7 us
    ppermute x7, starting transfers between devices, from_behind(): lax.ppermute(value, axis, [(source, source + steps) for source in range(l...  51.6 us
    all_to_all x1, waiting for transfers between devices, cross_attention(): lax.all_to_all(outgoing, 'seq', split_axis=0, concat_axis=0, tiled=True)  12.4 us
    unnamed x46, local copies, waits for them, and re-layouts  11.9 us
    all_to_all x1, starting transfers between devices, cross_attention(): lax.all_to_all(asked_slots, 'seq', split_axis=0, concat_axis=0, tiled=True)  7.28 us
    dot_general x1, matrix products, per_device(): jnp.dot(attended, out_weight, preferred_element_type=jnp.float32)  6.69 us
  transfers between devices with their start and end apart: 12, of which 11 were waited for; matrix products, arithmetic and copies ran while one was open for 11% of the time, Pallas kernels for 0%

commit v1 on v0

--- a/solution.py
+++ b/solution.py
@@ -6,6 +6,22 @@
 HEAD = 128
 SPAN = 64
 NEG_FILL = -1e30
+
+
+def swapped_with_each(x, axis, split, join):
+    ways, here = (lax.axis_size(axis), lax.axis_index(axis))
+    width = x.shape[split] // ways
+    shape = list(x.shape)
+    shape[split] = width
+    height = shape[join]
+    shape[join] = height * ways
+    full = jnp.zeros(shape, x.dtype)
+    for mask in range(ways):
+        part = lax.dynamic_slice_in_dim(x, (here ^ mask) * width, width, axis=split)
+        if mask:
+            part = lax.ppermute(part, axis, [(d, d ^ mask) for d in range(ways)])
+        full = lax.dynamic_update_slice_in_dim(full, part, (here ^ mask) * height, axis=join)
+    return full
 
 
 def from_behind(value, axis, steps):
@@ -119,7 +135,7 @@
         devices, capacity
     )
     asked = lax.all_to_all(outgoing, "seq", split_axis=0, concat_axis=0, tiled=True)
-    wanted = lax.all_to_all(asked_slots, "seq", split_axis=0, concat_axis=0, tiled=True)
+    wanted = swapped_with_each(asked_slots, "seq", 0, 0)
     source_count = wanted.shape[0]
     item_count = wanted.shape[1]
     key_heads = split_heads(memory_keys[wanted], HEAD)

time: 321 us -> 311 us (0.969)
  waiting for transfers between devices: 174 us -> 154 us
  starting transfers between devices: 71 us -> 82 us
    ppermute x0 -> x7, starting transfers between devices: none -> 13.5 us  [swapped_with_each(): part = lax.ppermute(part, axis, [(d, d ^ mask) for d in range(ways)])]
    all_to_all x1, waiting for transfers between devices: 12.4 us -> 0.01 us  [cross_attention(): lax.all_to_all(outgoing, 'seq', split_axis=0, concat_axis=0, tiled=True)]
    ppermute x7, waiting for transfers between devices: 105 us -> 93.7 us  [from_behind(): lax.ppermute(value, axis, [(source, source + steps) for source in range(l...]
    all_to_all x1 -> x0, starting transfers between devices: 7.28 us -> none  [cross_attention(): lax.all_to_all(asked_slots, 'seq', split_axis=0, concat_axis=0, tiled=True)]
    ppermute x0 -> x7, waiting for transfers between devices: none -> 6.82 us  [swapped_with_each(): part = lax.ppermute(part, axis, [(d, d ^ mask) for d in range(ways)])]
    unnamed x46 -> x48, local copies, waits for them, and re-layouts: 11.9 us -> 11.3 us
  transfers between devices with their start and end apart: 12 -> 18, of which waited for: 11 -> 14; matrix products, arithmetic and copies ran while one was open for 11% -> 11% of each run, Pallas kernels for 0% -> 0%
where the time goes in v1:
time: 311 us
  waiting for transfers between devices  154 us (50%)
  starting transfers between devices  82 us (26%)
  local copies, waits for them, and re-layouts  32.5 us (10%)
  matrix products  22.9 us (7%)
  between operations  13.8 us (4%)
  other arithmetic  4.82 us (2%)
    ppermute x7, waiting for transfers between devices, from_behind(): lax.ppermute(value, axis, [(source, source + steps) for source in range(l...  93.7 us
    ppermute x7, starting transfers between devices, from_behind(): lax.ppermute(value, axis, [(source, source + steps) for source in range(l...  51.5 us
    reduce_scatter x1, waiting for transfers between devices, per_device(): lax.psum_scatter(partial_value.astype(jnp.bfloat16), 'mp', scatter_dimens...  51.3 us
    ppermute x7, starting transfers between devices, swapped_with_each(): part = lax.ppermute(part, axis, [(d, d ^ mask) for d in range(ways)])  13.5 us
    unnamed x48, local copies, waits for them, and re-layouts  11.3 us
    all_to_all x1, starting transfers between devices, cross_attention(): lax.all_to_all(outgoing, 'seq', split_axis=0, concat_axis=0, tiled=True)  7.41 us
    ppermute x7, waiting for transfers between devices, swapped_with_each(): part = lax.ppermute(part, axis, [(d, d ^ mask) for d in range(ways)])  6.82 us
    dot_general x1, matrix products, per_device(): jnp.dot(attended, out_weight, preferred_element_type=jnp.float32)  6.67 us
  transfers between devices with their start and end apart: 18, of which 14 were waited for; matrix products, arithmetic and copies ran while one was open for 11% of the time, Pallas kernels for 0%

profile of v1, /device:TPU:0, one launch (start us, length us, event | category | flops | bytes accessed | tf_op | source)
XLA Modules:
  0.0 310.7 jit_solution(15144273376714077580)
XLA Ops:
  11.9 7.4 %all-to-all-start = ((bf16[8,2,64,512]{3,2,1,0:T(8,128)(2,1)}), bf16[8,2,64,512]{3,2,1,0:T(8,128)(2,1)}, u32[]{:S(2)}, u32[]{:S(2)}) async-start(bf16[8,2,64,512]{3,2,1,0:T(8,128)(2,1)} %bitcast.37), calls=%async_computation | async-start | bytes 2097152 | tf_op jit(solution)/shard_map/all_to_all | solution.py:137
  19.7 4.8 %collective-permute-start.7 = (s32[1,2]{1,0:T(1,128)S(1)}, s32[1,2]{1,0:T(1,128)S(1)}, u32[]{:S(2)}, u32[]{:S(2)}) collective-permute-start(s32[1,2]{1,0:T(1,128)S(1)} %get-tuple-element.248), channel_id=1, source_target_pairs={{0,28},{4,24},{8,20},{12,16},{16,12},{20,8},{24,4},{28,0},{1,29},{... | collective-permute-start | bytes 32 | tf_op jit(solution)/shard_map/ppermute | solution.py:22
  52.9 3.6 %multiply_reduce_fusion.2 = (f32[8,2,4,64]{3,2,1,0:T(4,128)S(1)}, f32[8,2,4,64,128]{4,3,2,1,0:T(8,128)S(1)}) fusion(bf16[8,2,128,4,128]{4,3,2,1,0:T(4,128)(2,1)} %reshape.124, bf16[8,2,64,512]{3,2,1,0:T(8,128)(2,1)} %all-to-all-done), kind=kOutput, calls=%fused_computation.28 | convolution fusion | flops 135262208 | bytes 5259264 | tf_op jit(solution)/shard_map/nicha,nikha->nihck/dot_general | solution.py:144
  60.5 5.1 %all-to-all-start.1 = ((bf16[8,2,256]{2,1,0:T(2,128)(2,1)}), bf16[8,2,256]{2,1,0:T(2,128)(2,1)S(1)}, u32[]{:S(2)}, u32[]{:S(2)}) async-start(bf16[8,2,256]{2,1,0:T(2,128)(2,1)} %reshape.154), calls=%async_computation.1 | async-start | bytes 16384 | tf_op jit(solution)/shard_map/all_to_all | solution.py:160
  72.1 4.2 %all-to-all-start.2 = ((bf16[8,2,64,512]{3,2,1,0:T(8,128)(2,1)}), bf16[8,2,64,512]{3,2,1,0:T(8,128)(2,1)}, u32[]{:S(2)}, u32[]{:S(2)}) async-start(bf16[8,2,64,512]{3,2,1,0:T(8,128)(2,1)} %bitcast.113), calls=%async_computation.2 | async-start | bytes 2097152 | tf_op jit(solution)/shard_map/all_to_all | solution.py:159
  80.1 151.6 %while.21 = (s32[]{:T(128)}, bf16[2,384,512]{1,2,0:T(8,128)(2,1)}, f32[4,384]{1,0:T(4,128)S(1)}, f32[4,384]{1,0:T(4,128)S(1)}, f32[4,384,128]{2,1,0:T(8,128)S(1)...) while((s32[]{:T(128)}, bf16[2,384,512]{1,2,0:T(8,128)(2,1)}, ...), condition=%wide.region_7.8_spmd, body=%wide.region_2.7_spmd.sunk | while | flops 307104768 | bytes 16220540 | solution.py:100
  80.2 3.6 %collective-permute-start = (bf16[2,384,512]{1,2,0:T(8,128)(2,1)}, bf16[2,384,512]{1,2,0:T(8,128)(2,1)S(1)}, u32[]{:S(2)}, u32[]{:S(2)}) collective-permute-start(bf16[2,384,512]{1,2,0:T(8,128)(2,1)} %get-tuple-element.329), channel_id=1, source_target_pairs={{0,4},{4,8},{8,12},{12,16},{16,20},{20,24},{24,28},{1,5},{5,9},{9,... | collective-permute-start | bytes 2359304 | tf_op jit(solution)/shard_map/while/body/eval_jaxpr/ppermute | solution.py:30
  83.8 19.2 %collective-permute-done = bf16[2,384,512]{1,2,0:T(8,128)(2,1)S(1)} collective-permute-done((bf16[2,384,512]{1,2,0:T(8,128)(2,1)}, bf16[2,384,512]{1,2,0:T(8,128)(2,1)S(1)}, u32[]{:S(2)}, u32[]{:S(2)}) %collective-permute-start) | collective-permute-done | bytes 786464 | tf_op jit(solution)/shard_map/while/body/eval_jaxpr/ppermute | solution.py:30
  103.9 10.5 %collective-permute-start = (bf16[2,384,512]{1,2,0:T(8,128)(2,1)}, bf16[2,384,512]{1,2,0:T(8,128)(2,1)S(1)}, u32[]{:S(2)}, u32[]{:S(2)}) collective-permute-start(bf16[2,384,512]{1,2,0:T(8,128)(2,1)} %get-tuple-element.329), channel_id=1, source_target_pairs={{0,4},{4,8},{8,12},{12,16},{16,20},{20,24},{24,28},{1,5},{5,9},{9,... | collective-permute-start | bytes 2359304 | tf_op jit(solution)/shard_map/while/body/eval_jaxpr/ppermute | solution.py:30
  114.4 12.7 %collective-permute-done = bf16[2,384,512]{1,2,0:T(8,128)(2,1)S(1)} collective-permute-done((bf16[2,384,512]{1,2,0:T(8,128)(2,1)}, bf16[2,384,512]{1,2,0:T(8,128)(2,1)S(1)}, u32[]{:S(2)}, u32[]{:S(2)}) %collective-permute-start) | collective-permute-done | bytes 786464 | tf_op jit(solution)/shard_map/while/body/eval_jaxpr/ppermute | solution.py:30
  128.0 5.2 %collective-permute-start = (bf16[2,384,512]{1,2,0:T(8,128)(2,1)}, bf16[2,384,512]{1,2,0:T(8,128)(2,1)S(1)}, u32[]{:S(2)}, u32[]{:S(2)}) collective-permute-start(bf16[2,384,512]{1,2,0:T(8,128)(2,1)} %get-tuple-element.329), channel_id=1, source_target_pairs={{0,4},{4,8},{8,12},{12,16},{16,20},{20,24},{24,28},{1,5},{5,9},{9,... | collective-permute-start | bytes 2359304 | tf_op jit(solution)/shard_map/while/body/eval_jaxpr/ppermute | solution.py:30
  133.3 11.8 %collective-permute-done = bf16[2,384,512]{1,2,0:T(8,128)(2,1)S(1)} collective-permute-done((bf16[2,384,512]{1,2,0:T(8,128)(2,1)}, bf16[2,384,512]{1,2,0:T(8,128)(2,1)S(1)}, u32[]{:S(2)}, u32[]{:S(2)}) %collective-permute-start) | collective-permute-done | bytes 786464 | tf_op jit(solution)/shard_map/while/body/eval_jaxpr/ppermute | solution.py:30
  145.9 14.5 %collective-permute-start = (bf16[2,384,512]{1,2,0:T(8,128)(2,1)}, bf16[2,384,512]{1,2,0:T(8,128)(2,1)S(1)}, u32[]{:S(2)}, u32[]{:S(2)}) collective-permute-start(bf16[2,384,512]{1,2,0:T(8,128)(2,1)} %get-tuple-element.329), channel_id=1, source_target_pairs={{0,4},{4,8},{8,12},{12,16},{16,20},{20,24},{24,28},{1,5},{5,9},{9,... | collective-permute-start | bytes 2359304 | tf_op jit(solution)/shard_map/while/body/eval_jaxpr/ppermute | solution.py:30
  160.4 13.9 %collective-permute-done = bf16[2,384,512]{1,2,0:T(8,128)(2,1)S(1)} collective-permute-done((bf16[2,384,512]{1,2,0:T(8,128)(2,1)}, bf16[2,384,512]{1,2,0:T(8,128)(2,1)S(1)}, u32[]{:S(2)}, u32[]{:S(2)}) %collective-permute-start) | collective-permute-done | bytes 786464 | tf_op jit(solution)/shard_map/while/body/eval_jaxpr/ppermute | solution.py:30
  175.2 5.2 %collective-permute-start = (bf16[2,384,512]{1,2,0:T(8,128)(2,1)}, bf16[2,384,512]{1,2,0:T(8,128)(2,1)S(1)}, u32[]{:S(2)}, u32[]{:S(2)}) collective-permute-start(bf16[2,384,512]{1,2,0:T(8,128)(2,1)} %get-tuple-element.329), channel_id=1, source_target_pairs={{0,4},{4,8},{8,12},{12,16},{16,20},{20,24},{24,28},{1,5},{5,9},{9,... | collective-permute-start | bytes 2359304 | tf_op jit(solution)/shard_map/while/body/eval_jaxpr/ppermute | solution.py:30
  180.5 13.0 %collective-permute-done = bf16[2,384,512]{1,2,0:T(8,128)(2,1)S(1)} collective-permute-done((bf16[2,384,512]{1,2,0:T(8,128)(2,1)}, bf16[2,384,512]{1,2,0:T(8,128)(2,1)S(1)}, u32[]{:S(2)}, u32[]{:S(2)}) %collective-permute-start) | collective-permute-done | bytes 786464 | tf_op jit(solution)/shard_map/while/body/eval_jaxpr/ppermute | solution.py:30
  194.3 7.2 %collective-permute-start = (bf16[2,384,512]{1,2,0:T(8,128)(2,1)}, bf16[2,384,512]{1,2,0:T(8,128)(2,1)S(1)}, u32[]{:S(2)}, u32[]{:S(2)}) collective-permute-start(bf16[2,384,512]{1,2,0:T(8,128)(2,1)} %get-tuple-element.329), channel_id=1, source_target_pairs={{0,4},{4,8},{8,12},{12,16},{16,20},{20,24},{24,28},{1,5},{5,9},{9,... | collective-permute-start | bytes 2359304 | tf_op jit(solution)/shard_map/while/body/eval_jaxpr/ppermute | solution.py:30
  201.5 12.0 %collective-permute-done = bf16[2,384,512]{1,2,0:T(8,128)(2,1)S(1)} collective-permute-done((bf16[2,384,512]{1,2,0:T(8,128)(2,1)}, bf16[2,384,512]{1,2,0:T(8,128)(2,1)S(1)}, u32[]{:S(2)}, u32[]{:S(2)}) %collective-permute-start) | collective-permute-done | bytes 786464 | tf_op jit(solution)/shard_map/while/body/eval_jaxpr/ppermute | solution.py:30
  214.5 5.2 %collective-permute-start = (bf16[2,384,512]{1,2,0:T(8,128)(2,1)}, bf16[2,384,512]{1,2,0:T(8,128)(2,1)S(1)}, u32[]{:S(2)}, u32[]{:S(2)}) collective-permute-start(bf16[2,384,512]{1,2,0:T(8,128)(2,1)} %get-tuple-element.329), channel_id=1, source_target_pairs={{0,4},{4,8},{8,12},{12,16},{16,20},{20,24},{24,28},{1,5},{5,9},{9,... | collective-permute-start | bytes 2359304 | tf_op jit(solution)/shard_map/while/body/eval_jaxpr/ppermute | solution.py:30
  219.7 11.1 %collective-permute-done = bf16[2,384,512]{1,2,0:T(8,128)(2,1)S(1)} collective-permute-done((bf16[2,384,512]{1,2,0:T(8,128)(2,1)}, bf16[2,384,512]{1,2,0:T(8,128)(2,1)S(1)}, u32[]{:S(2)}, u32[]{:S(2)}) %collective-permute-start) | collective-permute-done | bytes 786464 | tf_op jit(solution)/shard_map/while/body/eval_jaxpr/ppermute | solution.py:30
  232.1 6.7 %fusion.65 = f32[384,4096]{1,0:T(8,128)} fusion(bf16[384,512]{0,1:T(8,128)(2,1)S(1)} %bitcast.123, bf16[512,4096]{1,0:T(8,128)(2,1)} %param.22), kind=kOutput, calls=%fused_computation.97 | convolution fusion | flops 1610612736 | bytes 10878976 | tf_op jit(solution)/shard_map/dot_general | solution.py:198
  239.6 2.8 copy.130
  248.9 3.6 %add_convert_fusion = bf16[384,4096]{1,0:T(8,128)(2,1)} fusion(f32[384,4096]{1,0:T(8,128)S(1)} %bitcast.117, bf16[512,4096]{1,0:T(8,128)(2,1)S(1)} %copy-done.2, bf16[48,8,4,128]{3,2,1,0:T(4,128)(2,1)S(1)} %bitcast.120), kind=kOutput, calls=%fused_computation.16 | convolution fusion | flops 1613758464 | bytes 14024704 | tf_op jit(solution)/shard_map/dot_general | solution.py:199
  252.5 51.3 %reduce-scatter.2.cloned.1.call-done = bf16[384,1024]{1,0:T(8,128)(2,1)} async-done(((bf16[384,4096]{1,0:T(8,128)(2,1)}), bf16[384,1024]{1,0:T(8,128)(2,1)}) %reduce-scatter.2.cloned.1.call-update) | async-done | bytes 786448 | tf_op jit(solution)/shard_map/reduce_scatter | solution.py:202
  (135 shorter events, 62.0 us)
Async XLA Ops:
  6.5 39.6 %copy-start = (bf16[8,128,512]{2,1,0:T(8,128)(2,1)S(1)}, bf16[8,128,512]{2,1,0:T(8,128)(2,1)}, u32[]{:S(2)}) copy-start(bf16[8,128,512]{2,1,0:T(8,128)(2,1)} %param.19) | copy-start | bytes 3145732
  10.4 8.9 %copy-start.17 = (s32[6,2]{0,1:T(2,128)S(1)}, s32[6,2]{0,1:T(2,128)}, u32[]{:S(2)}) copy-start(s32[6,2]{0,1:T(2,128)} %param.21) | copy-start | bytes 148
  10.5 17.8 %copy-start.8 = (bf16[384,512]{1,0:T(8,128)(2,1)S(1)}, bf16[384,512]{1,0:T(8,128)(2,1)}, u32[]{:S(2)}) copy-start(bf16[384,512]{1,0:T(8,128)(2,1)} %param.15) | copy-start | bytes 1179652
  10.5 18.7 %copy-start.9 = (bf16[384,512]{1,0:T(8,128)(2,1)S(1)}, bf16[384,512]{1,0:T(8,128)(2,1)}, u32[]{:S(2)}) copy-start(bf16[384,512]{1,0:T(8,128)(2,1)} %param.16) | copy-start | bytes 1179652
  11.9 18.3 %copy-start.1 = (bf16[384,512]{1,0:T(8,128)(2,1)S(1)}, bf16[384,512]{1,0:T(8,128)(2,1)}, u32[]{:S(2)}) copy-start(bf16[384,512]{1,0:T(8,128)(2,1)} %param.14) | copy-start | bytes 1179652
  11.9 41.0 %all-to-all-start = ((bf16[8,2,64,512]{3,2,1,0:T(8,128)(2,1)}), bf16[8,2,64,512]{3,2,1,0:T(8,128)(2,1)}, u32[]{:S(2)}, u32[]{:S(2)}) async-start(bf16[8,2,64,512]{3,2,1,0:T(8,128)(2,1)} %bitcast.37), calls=%async_computation | async-start | bytes 2097152 | tf_op jit(solution)/shard_map/all_to_all | solution.py:137
  19.7 26.4 %collective-permute-start.7 = (s32[1,2]{1,0:T(1,128)S(1)}, s32[1,2]{1,0:T(1,128)S(1)}, u32[]{:S(2)}, u32[]{:S(2)}) collective-permute-start(s32[1,2]{1,0:T(1,128)S(1)} %get-tuple-element.248), channel_id=1, source_target_pairs={{0,28},{4,24},{8,20},{12,16},{16,12},{20,8},{24,4},{28,0},{1,29},{... | collective-permute-start | bytes 32 | tf_op jit(solution)/shard_map/ppermute | solution.py:22
  24.5 21.5 %collective-permute-start.6 = (s32[1,2]{1,0:T(1,128)S(1)}, s32[1,2]{1,0:T(1,128)S(1)}, u32[]{:S(2)}, u32[]{:S(2)}) collective-permute-start(s32[1,2]{1,0:T(1,128)S(1)} %get-tuple-element.249), channel_id=1, source_target_pairs={{0,24},{4,28},{8,16},{12,20},{16,8},{20,12},{24,0},{28,4},{1,25},{... | collective-permute-start | bytes 32 | tf_op jit(solution)/shard_map/ppermute | solution.py:22
  25.0 21.0 %collective-permute-start.5 = (s32[1,2]{1,0:T(1,128)S(1)}, s32[1,2]{1,0:T(1,128)S(1)}, u32[]{:S(2)}, u32[]{:S(2)}) collective-permute-start(s32[1,2]{1,0:T(1,128)S(1)} %get-tuple-element.250), channel_id=1, source_target_pairs={{0,20},{4,16},{8,28},{12,24},{16,4},{20,0},{24,12},{28,8},{1,21},{... | collective-permute-start | bytes 32 | tf_op jit(solution)/shard_map/ppermute | solution.py:22
  25.6 19.6 %collective-permute-start.4 = (s32[1,2]{1,0:T(1,128)S(1)}, s32[1,2]{1,0:T(1,128)S(1)}, u32[]{:S(2)}, u32[]{:S(2)}) collective-permute-start(s32[1,2]{1,0:T(1,128)S(1)} %get-tuple-element.251), channel_id=1, source_target_pairs={{0,16},{4,20},{8,24},{12,28},{16,0},{20,4},{24,8},{28,12},{1,17},{... | collective-permute-start | bytes 32 | tf_op jit(solution)/shard_map/ppermute | solution.py:22
  30.8 15.4 %copy-start.14 = (f32[4,384]{1,0:T(4,128)}, f32[4,384]{1,0:T(4,128)S(1)}, u32[]{:S(2)}) copy-start(f32[4,384]{1,0:T(4,128)S(1)} %get-tuple-element.256) | copy-start | bytes 18436
  33.3 3.5 %collective-permute-start.1 = (s32[1,2]{1,0:T(1,128)S(1)}, s32[1,2]{1,0:T(1,128)S(1)}, u32[]{:S(2)}, u32[]{:S(2)}) collective-permute-start(s32[1,2]{1,0:T(1,128)S(1)} %get-tuple-element.254), channel_id=1, source_target_pairs={{0,4},{4,0},{8,12},{12,8},{16,20},{20,16},{24,28},{28,24},{1,5},{5... | collective-permute-start | bytes 32 | tf_op jit(solution)/shard_map/ppermute | solution.py:22
  36.9 3.6 %collective-permute-start.2 = (s32[1,2]{1,0:T(1,128)S(1)}, s32[1,2]{1,0:T(1,128)S(1)}, u32[]{:S(2)}, u32[]{:S(2)}) collective-permute-start(s32[1,2]{1,0:T(1,128)S(1)} %get-tuple-element.253), channel_id=1, source_target_pairs={{0,8},{4,12},{8,0},{12,4},{16,24},{20,28},{24,16},{28,20},{1,9},{5... | collective-permute-start | bytes 32 | tf_op jit(solution)/shard_map/ppermute | solution.py:22
  40.5 4.6 %collective-permute-start.3 = (s32[1,2]{1,0:T(1,128)S(1)}, s32[1,2]{1,0:T(1,128)S(1)}, u32[]{:S(2)}, u32[]{:S(2)}) collective-permute-start(s32[1,2]{1,0:T(1,128)S(1)} %get-tuple-element.252), channel_id=1, source_target_pairs={{0,12},{4,8},{8,4},{12,0},{16,28},{20,24},{24,20},{28,16},{1,13},{... | collective-permute-start | bytes 32 | tf_op jit(solution)/shard_map/ppermute | solution.py:22
  60.5 11.6 %all-to-all-start.1 = ((bf16[8,2,256]{2,1,0:T(2,128)(2,1)}), bf16[8,2,256]{2,1,0:T(2,128)(2,1)S(1)}, u32[]{:S(2)}, u32[]{:S(2)}) async-start(bf16[8,2,256]{2,1,0:T(2,128)(2,1)} %reshape.154), calls=%async_computation.1 | async-start | bytes 16384 | tf_op jit(solution)/shard_map/all_to_all | solution.py:160
  72.1 167.5 %all-to-all-start.2 = ((bf16[8,2,64,512]{3,2,1,0:T(8,128)(2,1)}), bf16[8,2,64,512]{3,2,1,0:T(8,128)(2,1)}, u32[]{:S(2)}, u32[]{:S(2)}) async-start(bf16[8,2,64,512]{3,2,1,0:T(8,128)(2,1)} %bitcast.113), calls=%async_computation.2 | async-start | bytes 2097152 | tf_op jit(solution)/shard_map/all_to_all | solution.py:159
  76.3 227.5 %reduce-scatter.2.cloned.1.call-start = ((), (), s32[]{:S(2)}) async-start(), calls=%async_computation.4 | async-start | bytes 3932160 | tf_op jit(solution)/shard_map/reduce_scatter | solution.py:202
  80.2 22.8 %collective-permute-start = (bf16[2,384,512]{1,2,0:T(8,128)(2,1)}, bf16[2,384,512]{1,2,0:T(8,128)(2,1)S(1)}, u32[]{:S(2)}, u32[]{:S(2)}) collective-permute-start(bf16[2,384,512]{1,2,0:T(8,128)(2,1)} %get-tuple-element.329), channel_id=1, source_target_pairs={{0,4},{4,8},{8,12},{12,16},{16,20},{20,24},{24,28},{1,5},{5,9},{9,... | collective-permute-start | bytes 2359304 | tf_op jit(solution)/shard_map/while/body/eval_jaxpr/ppermute | solution.py:30
  103.9 23.3 %collective-permute-start = (bf16[2,384,512]{1,2,0:T(8,128)(2,1)}, bf16[2,384,512]{1,2,0:T(8,128)(2,1)S(1)}, u32[]{:S(2)}, u32[]{:S(2)}) collective-permute-start(bf16[2,384,512]{1,2,0:T(8,128)(2,1)} %get-tuple-element.329), channel_id=1, source_target_pairs={{0,4},{4,8},{8,12},{12,16},{16,20},{20,24},{24,28},{1,5},{5,9},{9,... | collective-permute-start | bytes 2359304 | tf_op jit(solution)/shard_map/while/body/eval_jaxpr/ppermute | solution.py:30
  128.0 17.0 %collective-permute-start = (bf16[2,384,512]{1,2,0:T(8,128)(2,1)}, bf16[2,384,512]{1,2,0:T(8,128)(2,1)S(1)}, u32[]{:S(2)}, u32[]{:S(2)}) collective-permute-start(bf16[2,384,512]{1,2,0:T(8,128)(2,1)} %get-tuple-element.329), channel_id=1, source_target_pairs={{0,4},{4,8},{8,12},{12,16},{16,20},{20,24},{24,28},{1,5},{5,9},{9,... | collective-permute-start | bytes 2359304 | tf_op jit(solution)/shard_map/while/body/eval_jaxpr/ppermute | solution.py:30
  145.9 28.4 %collective-permute-start = (bf16[2,384,512]{1,2,0:T(8,128)(2,1)}, bf16[2,384,512]{1,2,0:T(8,128)(2,1)S(1)}, u32[]{:S(2)}, u32[]{:S(2)}) collective-permute-start(bf16[2,384,512]{1,2,0:T(8,128)(2,1)} %get-tuple-element.329), channel_id=1, source_target_pairs={{0,4},{4,8},{8,12},{12,16},{16,20},{20,24},{24,28},{1,5},{5,9},{9,... | collective-permute-start | bytes 2359304 | tf_op jit(solution)/shard_map/while/body/eval_jaxpr/ppermute | solution.py:30
  175.2 18.2 %collective-permute-start = (bf16[2,384,512]{1,2,0:T(8,128)(2,1)}, bf16[2,384,512]{1,2,0:T(8,128)(2,1)S(1)}, u32[]{:S(2)}, u32[]{:S(2)}) collective-permute-start(bf16[2,384,512]{1,2,0:T(8,128)(2,1)} %get-tuple-element.329), channel_id=1, source_target_pairs={{0,4},{4,8},{8,12},{12,16},{16,20},{20,24},{24,28},{1,5},{5,9},{9,... | collective-permute-start | bytes 2359304 | tf_op jit(solution)/shard_map/while/body/eval_jaxpr/ppermute | solution.py:30
  194.3 19.3 %collective-permute-start = (bf16[2,384,512]{1,2,0:T(8,128)(2,1)}, bf16[2,384,512]{1,2,0:T(8,128)(2,1)S(1)}, u32[]{:S(2)}, u32[]{:S(2)}) collective-permute-start(bf16[2,384,512]{1,2,0:T(8,128)(2,1)} %get-tuple-element.329), channel_id=1, source_target_pairs={{0,4},{4,8},{8,12},{12,16},{16,20},{20,24},{24,28},{1,5},{5,9},{9,... | collective-permute-start | bytes 2359304 | tf_op jit(solution)/shard_map/while/body/eval_jaxpr/ppermute | solution.py:30
  214.5 16.4 %collective-permute-start = (bf16[2,384,512]{1,2,0:T(8,128)(2,1)}, bf16[2,384,512]{1,2,0:T(8,128)(2,1)S(1)}, u32[]{:S(2)}, u32[]{:S(2)}) collective-permute-start(bf16[2,384,512]{1,2,0:T(8,128)(2,1)} %get-tuple-element.329), channel_id=1, source_target_pairs={{0,4},{4,8},{8,12},{12,16},{16,20},{20,24},{24,28},{1,5},{5,9},{9,... | collective-permute-start | bytes 2359304 | tf_op jit(solution)/shard_map/while/body/eval_jaxpr/ppermute | solution.py:30
  (14 other events, 74.8 us)
Sparse Core Ops, SparseCore 0:
  252.6 51.1 reduce-scatter.1
